TPU v7x, 1024 devices: a whole 4x4x32 slice. The times are simulated.
1024 devices in a mesh: fsdp: 64 (over y_hi, z), mp: 16 (over y_lo, x, core).
Axes of the slice: x: 4, y: 4 (y_hi: 2, y_lo: 2; y = y_hi * 2 + y_lo), z: 32, core: 2. Of those that a mesh axis runs over, the one named last changes fastest.
Arguments:
- attn_out: bfloat16 [2048, 16384], P('mp', 'fsdp'), may hold values from -0.125 to 0.125
- grad_out: bfloat16 [2048, 16384], P('fsdp', 'mp'), may hold values from -6 to 6
- weight: bfloat16 [16384, 16384], P('fsdp', 'mp'), may hold values from -0.046875 to 0.046875
Outputs:
- grad_in: bfloat16 [2048, 16384], P('mp', 'fsdp')
- grad_weight: float32 [16384, 16384], P('fsdp', 'mp')
All inputs are finite; a program needn't handle non-finite values.
Results may differ from a plain program's by a relative error of at most 0.001.
Values may be sent and summed in bfloat16 or wider, within the bound.
A program may use at most 32 MiB of HBM per device.

v0:
```python
import jax
import jax.numpy as jnp
from jax import lax
from jax.sharding import PartitionSpec as P


def contract_rows(left, right):
    return lax.dot_general(
        left, right, (((0,), (0,)), ((), ())), preferred_element_type=jnp.float32
    )


def weight_grad(attn_out, all_grads):
    all_feats = lax.all_gather(attn_out, "mp", axis=0, tiled=True)
    return contract_rows(all_feats, all_grads)


def input_grad(all_grads, weight):
    summed = lax.psum_scatter(
        lax.dot_general(
            all_grads, weight, (((1,), (1,)), ((), ())), preferred_element_type=jnp.float32
        ),
        "mp",
        scatter_dimension=0,
        tiled=True,
    )
    return summed.astype(jnp.bfloat16)


def local(attn_out, grad_out, weight):
    all_grads = lax.all_gather(grad_out, "fsdp", axis=0, tiled=True)
    grad_weight = weight_grad(attn_out, all_grads)
    grad_in = input_grad(all_grads, weight)
    return (grad_in, grad_weight)


def solution(mesh):
    return jax.shard_map(
        local,
        mesh=mesh,
        in_specs=(P("mp", "fsdp"), P("fsdp", "mp"), P("fsdp", "mp")),
        out_specs=(P("mp", "fsdp"), P("fsdp", "mp")),
        check_vma=False,
    )
```

profile of v0, /device:TPU:1, one launch (start us, length us, event | category | flops | bytes accessed | tf_op | source)
XLA Modules:
  0.0 446.8 jit_solution(3187224678750904721)
XLA Ops:
  7.2 0.0 copy-start
  7.2 0.0 all-gather.3.cloned.1.call-start
  7.2 0.7 all-gather.3.cloned.1.call-update
  7.9 0.0 all-gather.5.cloned.1.call-start
  8.0 0.7 all-gather.5.cloned.1.call-update
  8.7 0.0 reduce-scatter.2.cloned.1.call-start
  8.7 285.8 %all-gather.3.cloned.1.call-done = bf16[2048,1024]{1,0:T(8,128)(2,1)} async-done(((bf16[32,1024]{1,0:T(8,128)(2,1)}), bf16[2048,1024]{1,0:T(8,128)(2,1)}) %all-gather.3.cloned.1.call-update) | async-done | bytes 4194320 | tf_op jit(solution)/shard_map/all_gather | solution.py:31
  294.5 0.0 copy-done
  294.5 4.8 %fusion = f32[2048,256]{1,0:T(8,128)} fusion(bf16[2048,1024]{1,0:T(8,128)(2,1)} %all-gather.3.cloned.1.call-done, bf16[256,1024]{1,0:T(8,128)(2,1)S(1)} %copy-done), kind=kOutput, calls=%fused_computation | convolution fusion | flops 1073741824 | bytes 6815744 | tf_op jit(solution)/shard_map/dot_general | solution.py:20
  299.3 0.0 reduce-scatter.2.cloned.1.call-update
  299.3 56.0 %all-gather.5.cloned.1.call-done = bf16[2048,256]{1,0:T(8,128)(2,1)} async-done(((bf16[128,256]{1,0:T(8,128)(2,1)}), bf16[2048,256]{1,0:T(8,128)(2,1)}) %all-gather.5.cloned.1.call-update) | async-done | bytes 1048592 | tf_op jit(solution)/shard_map/all_gather | solution.py:14
  355.3 4.8 %fusion.1 = f32[256,1024]{1,0:T(8,128)} fusion(bf16[2048,256]{1,0:T(8,128)(2,1)} %all-gather.5.cloned.1.call-done, bf16[2048,1024]{1,0:T(8,128)(2,1)} %all-gather.3.cloned.1.call-done), kind=kOutput, calls=%fused_computation.1 | convolution fusion | flops 1073741824 | bytes 6291456 | tf_op jit(solution)/shard_map/dot_general | solution.py:8
  360.0 78.7 %reduce-scatter.2.cloned.1.call-done = f32[128,256]{1,0:T(8,128)} async-done(((f32[2048,256]{1,0:T(8,128)}), f32[128,256]{1,0:T(8,128)}) %reduce-scatter.2.cloned.1.call-update) | async-done | bytes 131088 | tf_op jit(solution)/shard_map/reduce_scatter | solution.py:19
  438.7 1.5 convert_element_type.3
Async XLA Ops:
  7.2 287.3 %copy-start = (bf16[256,1024]{1,0:T(8,128)(2,1)S(1)}, bf16[256,1024]{1,0:T(8,128)(2,1)}, u32[]{:S(2)}) copy-start(bf16[256,1024]{1,0:T(8,128)(2,1)} %param.5) | copy-start | bytes 1572868
  7.2 287.3 %all-gather.3.cloned.1.call-start = ((), (), s32[]{:S(2)}) async-start(), calls=%async_computation.1 | async-start | bytes 4259840 | tf_op jit(solution)/shard_map/all_gather | solution.py:31
  7.9 347.3 %all-gather.5.cloned.1.call-start = ((), (), s32[]{:S(2)}) async-start(), calls=%async_computation.3 | async-start | bytes 1114112 | tf_op jit(solution)/shard_map/all_gather | solution.py:14
  8.7 430.0 %reduce-scatter.2.cloned.1.call-start = ((), (), s32[]{:S(2)}) async-start(), calls=%async_computation.2 | async-start | bytes 2228224 | tf_op jit(solution)/shard_map/reduce_scatter | solution.py:19
Sparse Core Ops, SparseCore 0:
  12.3 282.1 all-gather.2
  297.2 58.0 all-gather.4
  358.7 79.9 reduce-scatter.1
where the time goes:
time: 447 us
  waiting for transfers between devices  422 us (94%)
  between operations  13.8 us (3%)
  matrix products  9.57 us (2%)
    all_gather x1, waiting for transfers between devices, local(): all_grads = lax.all_gather(grad_out, 'fsdp', axis=0, tiled=True)  286 us
    reduce_scatter x1, waiting for transfers between devices, input_grad(): lax.psum_scatter(lax.dot_general(all_grads, weight, (((1,), (1,)), ((), (...  78.7 us
    all_gather x1, waiting for transfers between devices, weight_grad(): all_feats = lax.all_gather(attn_out, 'mp', axis=0, tiled=True)  56 us
  transfers between devices with their start and end apart: 3, of which 3 were waited for; matrix products, arithmetic and copies ran while one was open for 2% of the time, Pallas kernels for 0%

commit v1 on v0

v1 whole, which is shorter than its diff:
```python
import functools

import jax
import jax.numpy as jnp
from jax import lax
from jax.experimental import pallas as pl
from jax.experimental.pallas import tpu as pltpu
from jax.sharding import PartitionSpec as P

MESH = pl.DeviceIdType.MESH
NZ = 32
NM = 16
TOK = 32
HALF = 16
FAR = NZ // 2


def kernel(
    attn_ref, grad_ref, w_ref, gin_ref, gw_ref,
    grads, feats, parts, landed, total,
    x_send, x_recv, r_send, r_recv, l_send, l_recv, a_send, a_recv, p_send, p_recv, o_sem,
):
    f, me = lax.axis_index("fsdp"), lax.axis_index("mp")
    z, yh = lax.rem(f, NZ), f // NZ
    right = yh * NZ + lax.rem(z + 1, NZ)
    left = yh * NZ + lax.rem(z + NZ - 1, NZ)
    partner = (1 - yh) * NZ + z

    barrier = pltpu.get_barrier_semaphore()
    for dev in (right, left, partner):
        pl.semaphore_signal(barrier, inc=1, device_id=(dev, me), device_id_type=MESH)
    for k in range(1, NM):
        pl.semaphore_signal(barrier, inc=1, device_id=(f, lax.rem(me + k, NM)), device_id_type=MESH)
    pl.semaphore_wait(barrier, 3 + NM - 1)

    def row(p, pos):
        half = lax.rem(yh + p, 2)
        return pl.multiple_of((half * NZ + pos) * TOK, TOK)

    def behind(s):
        return lax.rem(z - s + NZ, NZ)

    def ahead(s):
        return lax.rem(z + s, NZ)

    def ring(rightward, s, q):
        p, c = q // 2, q % 2
        pos = behind(s) if rightward else ahead(s)
        ref = grads.at[pl.ds(pl.multiple_of(row(p, pos) + c * HALF, HALF), HALF)]
        send, recv = (r_send, r_recv) if rightward else (l_send, l_recv)
        return pltpu.make_async_remote_copy(
            src_ref=ref, dst_ref=ref, send_sem=send.at[s, q], recv_sem=recv.at[s, q],
            device_id=(right if rightward else left, me), device_id_type=MESH,
        )

    def arrived(rightward, s, q):
        p, c = q // 2, q % 2
        pos = behind(s) if rightward else ahead(s)
        ref = grads.at[pl.ds(pl.multiple_of(row(p, pos) + c * HALF, HALF), HALF)]
        send, recv = (r_send, r_recv) if rightward else (l_send, l_recv)
        pltpu.make_async_remote_copy(
            src_ref=ref, dst_ref=ref, send_sem=send.at[s - 1, q], recv_sem=recv.at[s - 1, q],
            device_id=(right if rightward else left, me), device_id_type=MESH,
        ).wait_recv()

    def swap(c, p=0):
        ref = grads.at[pl.ds(pl.multiple_of(row(p, z) + c * HALF, HALF), HALF)]
        return pltpu.make_async_remote_copy(
            src_ref=ref, dst_ref=ref, send_sem=x_send.at[c], recv_sem=x_recv.at[c],
            device_id=(partner, me), device_id_type=MESH,
        )

    def feature(k):
        return pltpu.make_async_remote_copy(
            src_ref=attn_ref, dst_ref=feats.at[pl.ds(pl.multiple_of(me * 128, 128), 128)],
            send_sem=a_send.at[k], recv_sem=a_recv.at[k],
            device_id=(f, lax.rem(me + k, NM)), device_id_type=MESH,
        )

    def partial(p, pos):
        first = row(p, pos)
        owner = first // 128
        k = lax.rem(owner - me + NM, NM)
        j = lax.rem(pos, 4)
        return k, pltpu.make_async_remote_copy(
            src_ref=parts.at[pl.ds(first, TOK)],
            dst_ref=landed.at[k, pl.ds(pl.multiple_of(j * TOK, TOK), TOK)],
            send_sem=p_send.at[k, j], recv_sem=p_recv.at[k, j],
            device_id=(f, owner), device_id_type=MESH,
        )

    grads[pl.ds(row(0, z), TOK)] = grad_ref[...]
    for c in range(2):
        swap(c).start()
    for q in range(2):
        ring(True, 0, q).start()
        ring(False, 0, q).start()
    for k in range(1, NM):
        feature(k).start()
    feats[pl.ds(pl.multiple_of(me * 128, 128), 128)] = attn_ref[...]
    total[...] = jnp.zeros_like(total)
    for c in range(2):
        swap(c, 1).wait_recv()
        ring(True, 0, 2 + c).start()
        ring(False, 0, 2 + c).start()

    def both(s):
        return [(p, pos) for pos in (behind(s), ahead(s)) for p in (0, 1)]

    def rows_of(ref, pieces, cols=slice(None)):
        return jnp.concatenate([ref[pl.ds(row(p, pos), TOK), cols] for p, pos in pieces], axis=0)

    def input_part(pieces):
        out = lax.dot_general(
            rows_of(grads, pieces), w_ref[...], (((1,), (1,)), ((), ())),
            preferred_element_type=jnp.float32,
        )
        for i, (p, pos) in enumerate(pieces):
            parts[pl.ds(row(p, pos), TOK)] = out[i * TOK : (i + 1) * TOK]
        for p, pos in pieces:
            k, copy = partial(p, pos)

            @pl.when(k != 0)
            def _():
                copy.start()

    def weight_part(pieces, cols):
        total[:, cols] += lax.dot_general(
            rows_of(feats, pieces), rows_of(grads, pieces, cols), (((0,), (0,)), ((), ())),
            preferred_element_type=jnp.float32,
        )

    own = [(0, z), (1, z)]
    far = [(0, ahead(FAR)), (1, ahead(FAR))]
    low, high = slice(0, 512), slice(512, 1024)
    input_part(own)

    def forward(s, q, last_right, last_left):
        arrived(True, s, q)
        if not last_right:
            ring(True, s, q).start()
        arrived(False, s, q)
        if not last_left:
            ring(False, s, q).start()

    def early(s, _):
        for q in range(4):
            forward(s, q, False, False)
            if q == 1:
                @pl.when(s > 1)
                def _():
                    input_part(both(s - 1))
        return 0

    lax.fori_loop(1, 9, early, 0)

    for k in range(1, NM):
        feature(k).wait_recv()

    def late(s, _):
        done = both(2 * (s - 8) - 1) + both(2 * (s - 8))
        for q in range(4):
            arrived(True, s, q)
            ring(True, s, q).start()
            arrived(False, s, q)

            @pl.when(s < FAR - 1)
            def _():
                ring(False, s, q).start()

            if q == 0:
                input_part(both(s - 1))
            if q == 1:
                weight_part(done, low)
            if q == 2:
                weight_part(done, high)
        return 0

    lax.fori_loop(9, FAR, late, 0)
    input_part(both(FAR - 1))
    weight_part(both(FAR - 1) + own, low)
    weight_part(both(FAR - 1) + own, high)
    for q in range(4):
        arrived(True, FAR, q)
    input_part(far)
    weight_part(far, slice(0, 1024))
    out = pltpu.make_async_copy(total, gw_ref, o_sem)
    out.start()

    mine = pl.multiple_of(me * 128, 128)
    summed = parts[pl.ds(mine, 128)]
    for k in range(1, NM):
        for j in range(4):
            pltpu.make_async_remote_copy(
                src_ref=parts.at[pl.ds(0, TOK)], dst_ref=landed.at[k, pl.ds(j * TOK, TOK)],
                send_sem=p_send.at[k, j], recv_sem=p_recv.at[k, j],
                device_id=(f, lax.rem(me + k, NM)), device_id_type=MESH,
            ).wait()
        summed = summed + landed[k]
    gin_ref[...] = summed.astype(gin_ref.dtype)

    for c in range(2):
        swap(c).wait_send()
    for k in range(1, NM):
        feature(k).wait_send()

    def drain(s, _):
        for q in range(4):
            ring(True, s, q).wait_send()

            @pl.when(s < FAR - 1)
            def _():
                ring(False, s, q).wait_send()
        return 0

    lax.fori_loop(0, FAR, drain, 0)
    out.wait()


def local(attn_out, grad_out, weight):
    vmem = pl.BlockSpec(memory_space=pltpu.VMEM)
    return pl.pallas_call(
        kernel,
        out_shape=(
            jax.ShapeDtypeStruct((128, 256), jnp.bfloat16),
            jax.ShapeDtypeStruct((256, 1024), jnp.float32),
        ),
        in_specs=[vmem] * 3,
        out_specs=(vmem, pl.BlockSpec(memory_space=pl.ANY)),
        scratch_shapes=[
            pltpu.VMEM((2048, 1024), jnp.bfloat16),
            pltpu.VMEM((2048, 256), jnp.bfloat16),
            pltpu.VMEM((2048, 256), jnp.float32),
            pltpu.VMEM((NM, 128, 256), jnp.float32),
            pltpu.VMEM((256, 1024), jnp.float32),
            pltpu.SemaphoreType.DMA((2,)),
            pltpu.SemaphoreType.DMA((2,)),
            pltpu.SemaphoreType.DMA((FAR, 4)),
            pltpu.SemaphoreType.DMA((FAR, 4)),
            pltpu.SemaphoreType.DMA((FAR, 4)),
            pltpu.SemaphoreType.DMA((FAR, 4)),
            pltpu.SemaphoreType.DMA((NM,)),
            pltpu.SemaphoreType.DMA((NM,)),
            pltpu.SemaphoreType.DMA((NM, 4)),
            pltpu.SemaphoreType.DMA((NM, 4)),
            pltpu.SemaphoreType.DMA,
        ],
        compiler_params=pltpu.CompilerParams(
            collective_id=0, has_side_effects=True, vmem_limit_bytes=40 << 20
        ),
    )(attn_out, grad_out, weight)


def solution(mesh):
    return jax.shard_map(
        local,
        mesh=mesh,
        in_specs=(P("mp", "fsdp"), P("fsdp", "mp"), P("fsdp", "mp")),
        out_specs=(P("mp", "fsdp"), P("fsdp", "mp")),
        check_vma=False,
    )
```

time: 447 us -> 101 us (0.23)
  the two profiles are of different devices: /device:TPU:1 before, /device:TPU:12 now
where the time goes in v1:
time: 101 us
  Pallas kernels  95.8 us (95%)
  local copies, waits for them, and re-layouts  4.31 us (4%)
    pallas_call x1, Pallas kernels, local(): pl.pallas_call(kernel, out_shape=(jax.ShapeDtypeStruct((128, 256), jnp.bf...  95.8 us
    unnamed x8, local copies, waits for them, and re-layouts  4.31 us

profile of v1, /device:TPU:12, one launch (start us, length us, event | category | flops | bytes accessed | tf_op | source)
XLA Modules:
  0.0 100.7 jit_solution(5803288826597071534)
XLA Ops:
  0.6 0.0 copy-start
  0.6 1.0 %copy-done = bf16[256,1024]{1,0:T(8,128)(2,1)S(1)} copy-done((bf16[256,1024]{1,0:T(8,128)(2,1)S(1)}, bf16[256,1024]{1,0:T(8,128)(2,1)}, u32[]{:S(2)}) %copy-start) | copy-done | bytes 524312
  1.7 0.0 copy-start.1
  1.7 0.8 copy-done.1
  2.5 0.0 copy-start.2
  2.5 0.8 copy-done.2
  3.4 95.8 %shard_map.50 = (bf16[128,256]{1,0:T(8,128)(2,1)S(1)}, f32[256,1024]{1,0:T(8,128)S(1)}) custom-call(bf16[128,256]{1,0:T(8,128)(2,1)S(1)} %copy-done.1, bf16[32,1024]{1,0:T(8,128)(2,1)S(1)} %copy-done.2, bf16[256,1024]{1,0:T(8,128)(2,1)S(1)} %copy-done), custom_call_target="tpu_custom_call" | custom-call | tf_op jit(solution)/shard_map/pallas_call | solution.py:222
  99.1 0.6 copy.7
  99.8 1.0 copy.8
Async XLA Ops:
  0.6 1.0 %copy-start = (bf16[256,1024]{1,0:T(8,128)(2,1)S(1)}, bf16[256,1024]{1,0:T(8,128)(2,1)}, u32[]{:S(2)}) copy-start(bf16[256,1024]{1,0:T(8,128)(2,1)} %w_ref.1) | copy-start | bytes 1572868
  1.7 0.8 copy-start.1
  2.5 0.8 copy-start.2

commit v2 on v1

v2 whole, which is shorter than its diff:
```python
import functools

import jax
import jax.numpy as jnp
from jax import lax
from jax.experimental import pallas as pl
from jax.experimental.pallas import tpu as pltpu
from jax.sharding import PartitionSpec as P

MESH = pl.DeviceIdType.MESH
NZ = 32
NM = 16
CHIPS = NM // 2
TOK = 32
HALF = 16
FAR = NZ // 2


def kernel(
    attn_hbm, grad_hbm, w_hbm, gin_ref, gw_ref,
    grads, feats, w_ref, kept, given, taken, landed, total,
    i_sem, x_send, x_recv, r_send, r_recv, l_send, l_recv,
    a_send, a_recv, m_send, m_recv, e_send, e_recv, p_send, p_recv, o_sem,
):
    f, me = lax.axis_index("fsdp"), lax.axis_index("mp")
    z, yh = lax.rem(f, NZ), f // NZ
    chip, core = me // 2, lax.rem(me, 2)
    mate = chip * 2 + (1 - core)
    right = yh * NZ + lax.rem(z + 1, NZ)
    left = yh * NZ + lax.rem(z + NZ - 1, NZ)
    partner = (1 - yh) * NZ + z

    own_rows = pl.ds(pl.multiple_of(f * TOK, TOK), TOK)
    own_feats = pl.ds(pl.multiple_of(me * 128, 128), 128)
    fetch = [
        pltpu.make_async_copy(grad_hbm, grads.at[own_rows], i_sem.at[0]),
        pltpu.make_async_copy(attn_hbm, feats.at[own_feats], i_sem.at[1]),
        pltpu.make_async_copy(w_hbm, w_ref, i_sem.at[2]),
    ]
    for copy in fetch:
        copy.start()

    barrier = pltpu.get_barrier_semaphore()
    for dev in (right, left, partner):
        pl.semaphore_signal(barrier, inc=1, device_id=(dev, me), device_id_type=MESH)
    for k in range(1, NM):
        pl.semaphore_signal(barrier, inc=1, device_id=(f, lax.rem(me + k, NM)), device_id_type=MESH)
    pl.semaphore_wait(barrier, 3 + NM - 1)

    def token(half, pos):
        return pl.multiple_of((half * NZ + pos) * TOK, TOK)

    def row(p, pos):
        return token(lax.rem(yh + p, 2), pos)

    def behind(s):
        return lax.rem(z - s + NZ, NZ)

    def ahead(s):
        return lax.rem(z + s, NZ)

    def hop(rightward, at, s, q):
        p, c = q // 2, q % 2
        pos = behind(at) if rightward else ahead(at)
        ref = grads.at[pl.ds(pl.multiple_of(row(p, pos) + c * HALF, HALF), HALF)]
        send, recv = (r_send, r_recv) if rightward else (l_send, l_recv)
        return pltpu.make_async_remote_copy(
            src_ref=ref, dst_ref=ref, send_sem=send.at[s, q], recv_sem=recv.at[s, q],
            device_id=(right if rightward else left, me), device_id_type=MESH,
        )

    def ring(rightward, s, q):
        return hop(rightward, s, s, q)

    def arrived(rightward, s, q):
        hop(rightward, s, s - 1, q).wait_recv()

    def swap(c, p=0):
        ref = grads.at[pl.ds(pl.multiple_of(row(p, z) + c * HALF, HALF), HALF)]
        return pltpu.make_async_remote_copy(
            src_ref=ref, dst_ref=ref, send_sem=x_send.at[c], recv_sem=x_recv.at[c],
            device_id=(partner, me), device_id_type=MESH,
        )

    def feature(k, incoming=False):
        src = lax.rem(chip - k + CHIPS, CHIPS) * 2 + core if incoming else me
        ref = feats.at[pl.ds(pl.multiple_of(src * 128, 128), 128)]
        return pltpu.make_async_remote_copy(
            src_ref=ref, dst_ref=ref, send_sem=a_send.at[k], recv_sem=a_recv.at[k],
            device_id=(f, lax.rem(chip + k, CHIPS) * 2 + core), device_id_type=MESH,
        )

    def pass_on(k, incoming=False):
        src = lax.rem(chip - k + CHIPS, CHIPS) * 2 + (1 - core if incoming else core)
        ref = feats.at[pl.ds(pl.multiple_of(src * 128, 128), 128)]
        return pltpu.make_async_remote_copy(
            src_ref=ref, dst_ref=ref, send_sem=m_send.at[k], recv_sem=m_recv.at[k],
            device_id=(f, mate), device_id_type=MESH,
        )

    def exchange(s, rows):
        return pltpu.make_async_remote_copy(
            src_ref=given.at[s, pl.ds(0, rows)], dst_ref=taken.at[s, pl.ds(0, rows)],
            send_sem=e_send.at[s], recv_sem=e_recv.at[s],
            device_id=(f, mate), device_id_type=MESH,
        )

    def deliver(s, i, pos):
        owner = core * CHIPS + pos // 4
        j = lax.rem(pos, 4)
        return owner, pltpu.make_async_remote_copy(
            src_ref=kept.at[s, pl.ds(i * TOK, TOK)],
            dst_ref=landed.at[chip, pl.ds(pl.multiple_of(j * TOK, TOK), TOK)],
            send_sem=p_send.at[pos], recv_sem=p_recv.at[chip, j],
            device_id=(f, owner), device_id_type=MESH,
        )

    fetch[0].wait()
    for q in range(2):
        ring(True, 0, q).start()
        ring(False, 0, q).start()
    for c in range(2):
        swap(c).start()
    fetch[1].wait()
    fetch[2].wait()
    pass_on(0).start()
    total[...] = jnp.zeros_like(total)
    for c in range(2):
        swap(c, 1).wait_recv()
        ring(True, 0, 2 + c).start()
        ring(False, 0, 2 + c).start()

    def both(s):
        return [(p, pos) for pos in (behind(s), ahead(s)) for p in (0, 1)]

    def input_part(s, places):
        n = len(places) * TOK
        lhs = [grads[pl.ds(token(half, pos), TOK), :] for half in (core, 1 - core) for pos in places]
        out = lax.dot_general(
            jnp.concatenate(lhs, axis=0), w_ref[...], (((1,), (1,)), ((), ())),
            preferred_element_type=jnp.float32,
        )
        given[s, pl.ds(0, n)] = out[n:]
        exchange(s, n).start()
        kept[s, pl.ds(0, n)] = out[:n]

    def combine(s, places):
        n = len(places) * TOK
        exchange(s, n).wait_recv()
        kept[s, pl.ds(0, n)] += taken[s, pl.ds(0, n)]
        for i, pos in enumerate(places):
            owner, copy = deliver(s, i, pos)

            @pl.when(owner != me)
            def _():
                copy.start()

            @pl.when(owner == me)
            def _():
                landed[chip, pl.ds(pl.multiple_of(lax.rem(pos, 4) * TOK, TOK), TOK)] = kept[s, pl.ds(i * TOK, TOK)]

    def rows_of(ref, pieces, cols=slice(None)):
        return jnp.concatenate([ref[pl.ds(row(p, pos), TOK), cols] for p, pos in pieces], axis=0)

    def weight_part(pieces, cols):
        total[:, cols] += lax.dot_general(
            rows_of(feats, pieces), rows_of(grads, pieces, cols), (((0,), (0,)), ((), ())),
            preferred_element_type=jnp.float32,
        )

    def pair(s):
        return [behind(s), ahead(s)]

    own = [(0, z), (1, z)]
    far = [(0, ahead(FAR)), (1, ahead(FAR))]
    low, high = slice(0, 512), slice(512, 1024)
    input_part(0, [z])

    def early(s, _):
        for q in range(4):
            arrived(True, s, q)
            ring(True, s, q).start()
            arrived(False, s, q)
            ring(False, s, q).start()
            if q == 0:
                @pl.when(s > 2)
                def _():
                    combine(s - 2, pair(s - 2))

                @pl.when(s > 1)
                def _():
                    input_part(s - 1, pair(s - 1))
            if q % 2 == 1:
                k = 2 * (s - 1) + (q + 1) // 2

                @pl.when(k < CHIPS)
                def _():
                    feature(k).start()

                back = k - CHIPS

                @pl.when((back > 0) & (back < CHIPS))
                def _():
                    feature(back, True).wait_recv()
                    pass_on(back).start()
        return 0

    lax.fori_loop(1, 9, early, 0)

    combine(0, [z])
    for k in range(CHIPS):
        pass_on(k, True).wait_recv()

    def late(s, _):
        done = both(2 * (s - 8) - 1) + both(2 * (s - 8))
        for q in range(4):
            arrived(True, s, q)
            ring(True, s, q).start()
            arrived(False, s, q)

            @pl.when(s < FAR - 1)
            def _():
                ring(False, s, q).start()

            if q == 0:
                combine(s - 2, pair(s - 2))
                input_part(s - 1, pair(s - 1))
            if q == 1:
                weight_part(done, low)
            if q == 2:
                weight_part(done, high)
        return 0

    lax.fori_loop(9, FAR, late, 0)
    combine(FAR - 2, pair(FAR - 2))
    input_part(FAR - 1, pair(FAR - 1))
    weight_part(both(FAR - 1) + own, low)
    combine(FAR - 1, pair(FAR - 1))
    weight_part(both(FAR - 1) + own, high)
    for q in range(4):
        arrived(True, FAR, q)
    input_part(FAR, [ahead(FAR)])
    weight_part(far, slice(0, 1024))
    combine(FAR, [ahead(FAR)])
    out = pltpu.make_async_copy(total, gw_ref, o_sem)
    out.start()

    for c in range(CHIPS):
        for j in range(4):
            @pl.when((chip != c) | (core != me // CHIPS))
            def _():
                ref = landed.at[c, pl.ds(j * TOK, TOK)]
                pltpu.make_async_remote_copy(
                    src_ref=ref, dst_ref=ref, send_sem=p_send.at[0], recv_sem=p_recv.at[c, j],
                    device_id=(f, mate), device_id_type=MESH,
                ).wait_recv()
    summed = landed[0]
    for c in range(1, CHIPS):
        summed = summed + landed[c]
    gin_ref[...] = summed.astype(gin_ref.dtype)

    def sent(s, i, pos):
        owner, copy = deliver(s, i, pos)

        @pl.when(owner != me)
        def _():
            copy.wait_send()

    for c in range(2):
        swap(c).wait_send()
    pass_on(0).wait_send()
    for k in range(1, CHIPS):
        feature(k).wait_send()
        pass_on(k).wait_send()
    exchange(0, TOK).wait_send()
    exchange(FAR, TOK).wait_send()
    sent(0, 0, z)
    sent(FAR, 0, ahead(FAR))

    def drain(s, _):
        @pl.when(s > 0)
        def _():
            exchange(s, 2 * TOK).wait_send()
            for i, pos in enumerate(pair(s)):
                sent(s, i, pos)

        for q in range(4):
            ring(True, s, q).wait_send()

            @pl.when(s < FAR - 1)
            def _():
                ring(False, s, q).wait_send()
        return 0

    lax.fori_loop(0, FAR, drain, 0)
    out.wait()


def local(attn_out, grad_out, weight):
    vmem = pl.BlockSpec(memory_space=pltpu.VMEM)
    dma = pltpu.SemaphoreType.DMA
    args = [pltpu.with_memory_space_constraint(x, pltpu.HBM) for x in (attn_out, grad_out, weight)]
    return pl.pallas_call(
        kernel,
        out_shape=(
            jax.ShapeDtypeStruct((128, 256), jnp.bfloat16),
            jax.ShapeDtypeStruct((256, 1024), jnp.float32),
        ),
        in_specs=[pl.BlockSpec(memory_space=pltpu.HBM)] * 3,
        out_specs=(vmem, pl.BlockSpec(memory_space=pl.ANY)),
        scratch_shapes=[
            pltpu.VMEM((2048, 1024), jnp.bfloat16),
            pltpu.VMEM((2048, 256), jnp.bfloat16),
            pltpu.VMEM((256, 1024), jnp.bfloat16),
            pltpu.VMEM((FAR + 1, 2 * TOK, 256), jnp.float32),
            pltpu.VMEM((FAR + 1, 2 * TOK, 256), jnp.float32),
            pltpu.VMEM((FAR + 1, 2 * TOK, 256), jnp.float32),
            pltpu.VMEM((CHIPS, 128, 256), jnp.float32),
            pltpu.VMEM((256, 1024), jnp.float32),
            dma((3,)),
            dma((2,)),
            dma((2,)),
            dma((FAR, 4)),
            dma((FAR, 4)),
            dma((FAR, 4)),
            dma((FAR, 4)),
            dma((CHIPS,)),
            dma((CHIPS,)),
            dma((CHIPS,)),
            dma((CHIPS,)),
            dma((FAR + 1,)),
            dma((FAR + 1,)),
            dma((NZ,)),
            dma((CHIPS, 4)),
            dma,
        ],
        compiler_params=pltpu.CompilerParams(
            collective_id=0, has_side_effects=True, vmem_limit_bytes=40 << 20
        ),
    )(*args)


def solution(mesh):
    return jax.shard_map(
        local,
        mesh=mesh,
        in_specs=(P("mp", "fsdp"), P("fsdp", "mp"), P("fsdp", "mp")),
        out_specs=(P("mp", "fsdp"), P("fsdp", "mp")),
        check_vma=False,
    )
```

time: 101 us -> 90.9 us (0.900)
  the two profiles are of different devices: /device:TPU:12 before, /device:TPU:1 now
where the time goes in v2:
time: 90.9 us; the launch traced here: 90.8 us
  Pallas kernels  88.5 us (97%)
  local copies, waits for them, and re-layouts  1.6 us (2%)
    pallas_call x1, Pallas kernels, local(): pl.pallas_call(kernel, out_shape=(jax.ShapeDtypeStruct((128, 256), jnp.bf...  88.5 us

profile of v2, /device:TPU:1, one launch (start us, length us, event | category | flops | bytes accessed | tf_op | source)
XLA Modules:
  0.0 90.8 jit_solution(14052347233433419764)
XLA Ops:
  0.6 88.5 %shard_map.50 = (bf16[128,256]{1,0:T(8,128)(2,1)S(1)}, f32[256,1024]{1,0:T(8,128)S(1)}) custom-call(bf16[128,256]{1,0:T(8,128)(2,1)} %attn_hbm.1, bf16[32,1024]{1,0:T(8,128)(2,1)} %grad_hbm.1, bf16[256,1024]{1,0:T(8,128)(2,1)} %w_hbm.1), custom_call_target="tpu_custom_call" | custom-call | tf_op jit(solution)/shard_map/pallas_call | solution.py:303
  89.2 0.6 copy.7
  89.8 1.0 %copy.8 = f32[256,1024]{1,0:T(8,128)} copy(f32[256,1024]{1,0:T(8,128)S(1)} %get-tuple-element.5) | data formatting | bytes 2097152

commit v3 on v2

--- a/solution.py
+++ b/solution.py
@@ -17,17 +17,17 @@
 
 
 def kernel(
-    attn_hbm, grad_hbm, w_hbm, gin_ref, gw_ref,
-    grads, feats, w_ref, kept, given, taken, landed, total,
-    i_sem, x_send, x_recv, r_send, r_recv, l_send, l_recv,
-    a_send, a_recv, m_send, m_recv, e_send, e_recv, p_send, p_recv, o_sem,
+    attn_hbm, grad_hbm, w_hbm, gin_ref, total,
+    grads, feats, w_ref, kept, given, taken, landed,
+    i_sem, x_send, x_recv, d_send, d_recv, t_send, t_recv,
+    a_send, a_recv, m_send, m_recv, e_send, e_recv, p_send, p_recv,
 ):
     f, me = lax.axis_index("fsdp"), lax.axis_index("mp")
     z, yh = lax.rem(f, NZ), f // NZ
     chip, core = me // 2, lax.rem(me, 2)
     mate = chip * 2 + (1 - core)
-    right = yh * NZ + lax.rem(z + 1, NZ)
-    left = yh * NZ + lax.rem(z + NZ - 1, NZ)
+    down = yh * NZ + lax.rem(z + NZ - 1, NZ)
+    up = yh * NZ + lax.rem(z + 1, NZ)
     partner = (1 - yh) * NZ + z
 
     own_rows = pl.ds(pl.multiple_of(f * TOK, TOK), TOK)
@@ -41,7 +41,7 @@
         copy.start()
 
     barrier = pltpu.get_barrier_semaphore()
-    for dev in (right, left, partner):
+    for dev in (down, up, partner):
         pl.semaphore_signal(barrier, inc=1, device_id=(dev, me), device_id_type=MESH)
     for k in range(1, NM):
         pl.semaphore_signal(barrier, inc=1, device_id=(f, lax.rem(me + k, NM)), device_id_type=MESH)
@@ -53,27 +53,27 @@
     def row(p, pos):
         return token(lax.rem(yh + p, 2), pos)
 
-    def behind(s):
+    def above(s):
+        return lax.rem(z + s, NZ)
+
+    def below(s):
         return lax.rem(z - s + NZ, NZ)
 
-    def ahead(s):
-        return lax.rem(z + s, NZ)
-
-    def hop(rightward, at, s, q):
+    def hop(downward, at, s, q):
         p, c = q // 2, q % 2
-        pos = behind(at) if rightward else ahead(at)
+        pos = above(at) if downward else below(at)
         ref = grads.at[pl.ds(pl.multiple_of(row(p, pos) + c * HALF, HALF), HALF)]
-        send, recv = (r_send, r_recv) if rightward else (l_send, l_recv)
+        send, recv = (d_send, d_recv) if downward else (t_send, t_recv)
         return pltpu.make_async_remote_copy(
             src_ref=ref, dst_ref=ref, send_sem=send.at[s, q], recv_sem=recv.at[s, q],
-            device_id=(right if rightward else left, me), device_id_type=MESH,
-        )
-
-    def ring(rightward, s, q):
-        return hop(rightward, s, s, q)
-
-    def arrived(rightward, s, q):
-        hop(rightward, s, s - 1, q).wait_recv()
+            device_id=(down if downward else up, me), device_id_type=MESH,
+        )
+
+    def ring(downward, s, q):
+        return hop(downward, s, s, q)
+
+    def arrived(downward, s, q):
+        hop(downward, s, s - 1, q).wait_recv()
 
     def swap(c, p=0):
         ref = grads.at[pl.ds(pl.multiple_of(row(p, z) + c * HALF, HALF), HALF)]
@@ -131,7 +131,7 @@
         ring(False, 0, 2 + c).start()
 
     def both(s):
-        return [(p, pos) for pos in (behind(s), ahead(s)) for p in (0, 1)]
+        return [(p, pos) for pos in (above(s), below(s)) for p in (0, 1)]
 
     def input_part(s, places):
         n = len(places) * TOK
@@ -169,10 +169,10 @@
         )
 
     def pair(s):
-        return [behind(s), ahead(s)]
+        return [above(s), below(s)]
 
     own = [(0, z), (1, z)]
-    far = [(0, ahead(FAR)), (1, ahead(FAR))]
+    far = [(0, below(FAR)), (1, below(FAR))]
     low, high = slice(0, 512), slice(512, 1024)
     input_part(0, [z])
 
@@ -239,12 +239,42 @@
     weight_part(both(FAR - 1) + own, high)
     for q in range(4):
         arrived(True, FAR, q)
-    input_part(FAR, [ahead(FAR)])
+    input_part(FAR, [below(FAR)])
     weight_part(far, slice(0, 1024))
-    combine(FAR, [ahead(FAR)])
-    out = pltpu.make_async_copy(total, gw_ref, o_sem)
-    out.start()
-
+    combine(FAR, [below(FAR)])
+
+    def sent(s, i, pos):
+        owner, copy = deliver(s, i, pos)
+
+        @pl.when(owner != me)
+        def _():
+            copy.wait_send()
+
+    for c in range(2):
+        swap(c).wait_send()
+    pass_on(0).wait_send()
+    for k in range(1, CHIPS):
+        feature(k).wait_send()
+        pass_on(k).wait_send()
+    exchange(0, TOK).wait_send()
+    sent(0, 0, z)
+
+    def drain(s, _):
+        @pl.when((s > 0) & (s < FAR - 1))
+        def _():
+            exchange(s, 2 * TOK).wait_send()
+            for i, pos in enumerate(pair(s)):
+                sent(s, i, pos)
+
+        for q in range(4):
+            ring(True, s, q).wait_send()
+
+            @pl.when(s < FAR - 1)
+            def _():
+                ring(False, s, q).wait_send()
+        return 0
+
+    lax.fori_loop(0, FAR, drain, 0)
     for c in range(CHIPS):
         for j in range(4):
             @pl.when((chip != c) | (core != me // CHIPS))
@@ -259,41 +289,11 @@
         summed = summed + landed[c]
     gin_ref[...] = summed.astype(gin_ref.dtype)
 
-    def sent(s, i, pos):
-        owner, copy = deliver(s, i, pos)
-
-        @pl.when(owner != me)
-        def _():
-            copy.wait_send()
-
-    for c in range(2):
-        swap(c).wait_send()
-    pass_on(0).wait_send()
-    for k in range(1, CHIPS):
-        feature(k).wait_send()
-        pass_on(k).wait_send()
-    exchange(0, TOK).wait_send()
+    exchange(FAR - 1, 2 * TOK).wait_send()
     exchange(FAR, TOK).wait_send()
-    sent(0, 0, z)
-    sent(FAR, 0, ahead(FAR))
-
-    def drain(s, _):
-        @pl.when(s > 0)
-        def _():
-            exchange(s, 2 * TOK).wait_send()
-            for i, pos in enumerate(pair(s)):
-                sent(s, i, pos)
-
-        for q in range(4):
-            ring(True, s, q).wait_send()
-
-            @pl.when(s < FAR - 1)
-            def _():
-                ring(False, s, q).wait_send()
-        return 0
-
-    lax.fori_loop(0, FAR, drain, 0)
-    out.wait()
+    for i, pos in enumerate(pair(FAR - 1)):
+        sent(FAR - 1, i, pos)
+    sent(FAR, 0, below(FAR))
 
 
 def local(attn_out, grad_out, weight):
@@ -307,7 +307,7 @@
             jax.ShapeDtypeStruct((256, 1024), jnp.float32),
         ),
         in_specs=[pl.BlockSpec(memory_space=pltpu.HBM)] * 3,
-        out_specs=(vmem, pl.BlockSpec(memory_space=pl.ANY)),
+        out_specs=(vmem, vmem),
         scratch_shapes=[
             pltpu.VMEM((2048, 1024), jnp.bfloat16),
             pltpu.VMEM((2048, 256), jnp.bfloat16),
@@ -316,7 +316,6 @@
             pltpu.VMEM((FAR + 1, 2 * TOK, 256), jnp.float32),
             pltpu.VMEM((FAR + 1, 2 * TOK, 256), jnp.float32),
             pltpu.VMEM((CHIPS, 128, 256), jnp.float32),
-            pltpu.VMEM((256, 1024), jnp.float32),
             dma((3,)),
             dma((2,)),
             dma((2,)),
@@ -332,7 +331,6 @@
             dma((FAR + 1,)),
             dma((NZ,)),
             dma((CHIPS, 4)),
-            dma,
         ],
         compiler_params=pltpu.CompilerParams(
             collective_id=0, has_side_effects=True, vmem_limit_bytes=40 << 20

time: 90.9 us -> 88.7 us (0.976)
  Pallas kernels: 88.5 us -> 86.2 us
    pallas_call x1, Pallas kernels: 88.5 us -> 86.2 us  [local(): pl.pallas_call(kernel, out_shape=(jax.ShapeDtypeStruct((128, 256), jnp.bf...]
where the time goes in v3:
time: 88.7 us; the launch traced here: 88.4 us
  Pallas kernels  86.2 us (97%)
  local copies, waits for them, and re-layouts  1.6 us (2%)
    pallas_call x1, Pallas kernels, local(): pl.pallas_call(kernel, out_shape=(jax.ShapeDtypeStruct((128, 256), jnp.bf...  86.2 us

profile of v3, /device:TPU:1, one launch (start us, length us, event | category | flops | bytes accessed | tf_op | source)
XLA Modules:
  0.0 88.4 jit_solution(2338051726732108279)
XLA Ops:
  0.6 86.2 %shard_map.50 = (bf16[128,256]{1,0:T(8,128)(2,1)S(1)}, f32[256,1024]{1,0:T(8,128)S(1)}) custom-call(bf16[128,256]{1,0:T(8,128)(2,1)} %attn_hbm.1, bf16[32,1024]{1,0:T(8,128)(2,1)} %grad_hbm.1, bf16[256,1024]{1,0:T(8,128)(2,1)} %w_hbm.1), custom_call_target="tpu_custom_call" | custom-call | tf_op jit(solution)/shard_map/pallas_call | solution.py:303
  86.8 0.6 copy.7
  87.4 1.0 %copy.8 = f32[256,1024]{1,0:T(8,128)} copy(f32[256,1024]{1,0:T(8,128)S(1)} %get-tuple-element.5) | data formatting | bytes 2097152
